TPU v7x, 32 devices: a whole 2x2x4 slice. The times are simulated.
32 devices in a mesh: groups: 2 (over y), ctx: 4 (over z), tp: 2 (over x), dp: 2 (over core).
Axes of the slice: x: 2, y: 2, z: 4, core: 2. Of those that a mesh axis runs over, the one named last changes fastest.
Arguments:
- queries: bfloat16 [4, 1024, 4096], P(('groups', 'dp'), 'ctx', 'tp'), parts along dimension 0, may hold values from -27 to 27
- keys_values: bfloat16 [4, 2, 1024, 512], P(('groups', 'dp'), None, ('ctx', 'tp')), parts along dimension 0, may hold values from -9 to 9
- segment_ids: int32 [4, 1024], P(('groups', 'dp'), 'ctx'), parts along dimension 0, may hold values from 0 to 2, as said below
Outputs:
- attended: bfloat16 [4, 1024, 4096], P(('groups', 'dp'), 'ctx', 'tp'), parts along dimension 0
There are 2 independent parts, one for each index of `groups`. A program takes and returns all parts, laid end to end along the dimension named above; each array names one. Nothing has to cross between parts.
Inputs may be any that keep to these rules, and one draw needn't show every extreme that they name: `segment_ids`: ids never fall along rows; the rows of the first 3 indices of ctx form one trajectory with id 0; the rows of every other index of ctx hold one or two whole trajectories, the last index two.
All inputs are finite; a program needn't handle non-finite values.
Results may differ from a plain program's by a relative error of at most 0.0026.
Values may be sent and summed in bfloat16 or wider, within the bound.
A program may use at most 64 MiB of HBM per device.

v0:
```python
import functools
import math

import jax
import jax.numpy as jnp
from jax import lax
from jax.experimental import pallas as pl
from jax.experimental.pallas import tpu as pltpu
from jax.sharding import PartitionSpec as P

HEAD_DIM = 128
MESH = pl.DeviceIdType.MESH
LOG2_SCALE = math.log2(math.e) / math.sqrt(HEAD_DIM)


def kernel(n_long, n_tp, q_ref, kv_ref, seg_ref, out_ref, q_v, kv_v, bias_v, top_v, total_v, sum_v, out_v,
           send_sem, recv_sem, q_sem, out_sem):
    groups = kv_v.shape[2]
    rows = q_v.shape[0]
    part = kv_ref.shape[2]
    heads = q_v.shape[1] // HEAD_DIM
    per_group = heads // groups
    width = per_group * HEAD_DIM

    c = lax.axis_index("ctx")
    t = lax.axis_index("tp")
    is_long = c < n_long
    first = jnp.where(is_long, 0, c)
    end = jnp.where(is_long, n_long, c + 1)
    own = jnp.where(is_long, c, 0)

    def q_copy(g):
        columns = pl.ds(g * width, width)
        return pltpu.make_async_copy(q_ref.at[0, :, columns], q_v.at[:, columns], q_sem.at[g])

    def out_copy(g):
        columns = pl.ds(g * width, width)
        return pltpu.make_async_copy(out_v.at[:, columns], out_ref.at[0, :, columns], out_sem.at[g])

    def partner(o):
        return lax.rem(t + o, n_tp)

    def place(g, kv):
        return kv_v.at[own, kv, g, pl.ds(pl.multiple_of(t * part, part), part), :]

    def block(tp_index, g, kv):
        column = pl.multiple_of((tp_index * groups + g) * HEAD_DIM, HEAD_DIM)
        return kv_ref.at[0, kv, :, pl.ds(column, HEAD_DIM)]

    def local_copy(g, kv):
        return pltpu.make_async_copy(block(t, g, kv), place(g, kv), recv_sem.at[own, g, kv])

    def remote_copy(dest, distance, o, g, kv):
        return pltpu.make_async_remote_copy(
            src_ref=block(partner(o), g, kv),
            dst_ref=place(g, kv),
            send_sem=send_sem.at[distance, o, g, kv],
            recv_sem=recv_sem.at[own, g, kv],
            device_id={"ctx": dest, "tp": partner(o)},
            device_id_type=MESH,
        )

    barrier = pltpu.get_barrier_semaphore()
    for o in range(1, n_tp):
        pl.semaphore_signal(barrier, inc=1, device_id={"ctx": c, "tp": partner(o)}, device_id_type=MESH)

    def greet(source, carry):
        for o in range(n_tp):
            pl.semaphore_signal(barrier, inc=1, device_id={"ctx": source, "tp": partner(o)}, device_id_type=MESH)
        return carry

    lax.fori_loop(first, c, greet, 0)
    for g in range(groups):
        for kv in range(2):
            local_copy(g, kv).start()
        q_copy(g).start()
    pl.semaphore_wait(barrier, (end - c) * n_tp - 1)

    for g in range(groups):
        for kv in range(2):
            for o in range(1, n_tp):
                remote_copy(c, 0, o, g, kv).start()
    for g in range(groups):
        for kv in range(2):
            def send(i, carry, g=g, kv=kv):
                dest = end - 1 - i
                for o in range(n_tp):
                    remote_copy(dest, dest - c, o, g, kv).start()
                return carry

            lax.fori_loop(0, end - 1 - c, send, 0)

    seg = seg_ref[...]
    seg_rows = jnp.transpose(jnp.broadcast_to(seg.astype(jnp.float32), (HEAD_DIM, rows)))[:, :1].astype(jnp.int32)
    row_index = lax.broadcasted_iota(jnp.int32, (rows, rows), 0)
    key_index = lax.broadcasted_iota(jnp.int32, (rows, rows), 1)
    visible = (seg_rows == seg) & (key_index <= row_index)
    bias_v[...] = jnp.where(visible, 0.0, -1e30)

    def arrived(slot, g, kv):
        whole = kv_v.at[slot, kv, g]
        pltpu.make_async_copy(whole, whole, recv_sem.at[slot, g, kv]).wait()

    def scores_of(h, key_rows):
        q = q_v[:, pl.ds(pl.multiple_of(h * HEAD_DIM, HEAD_DIM), HEAD_DIM)]
        return lax.dot_general(q, key_rows, (((1,), (1,)), ((), ())), preferred_element_type=jnp.float32) * LOG2_SCALE

    for g in range(groups):
        q_copy(g).wait()
        arrived(own, g, 0)
        arrived(own, g, 1)

        def own_head(i, carry, g=g):
            h = g * per_group + i
            scores = scores_of(h, kv_v[own, 0, g]) + bias_v[...]
            top = jnp.max(scores, axis=1, keepdims=True)
            weights = jnp.exp2(scores - top)
            top_v[h] = jnp.broadcast_to(top, (rows, HEAD_DIM))
            total_v[h] = jnp.broadcast_to(jnp.sum(weights, axis=1, keepdims=True), (rows, HEAD_DIM))
            sum_v[h] = jnp.dot(weights.astype(jnp.bfloat16), kv_v[own, 1, g], preferred_element_type=jnp.float32)
            return carry

        lax.fori_loop(0, per_group, own_head, 0, unroll=2)

    for g in range(groups):
        def source_step(i, carry, g=g):
            slot = c - 1 - i
            arrived(slot, g, 0)
            arrived(slot, g, 1)

            def head(j, inner):
                h = g * per_group + j
                scores = scores_of(h, kv_v[slot, 0, g])
                old = top_v[h]
                top = jnp.maximum(old, jnp.max(scores, axis=1, keepdims=True))
                weights = jnp.exp2(scores - top[:, :1])
                factor = jnp.exp2(old - top)
                top_v[h] = top
                total_v[h] = total_v[h] * factor + jnp.sum(weights, axis=1, keepdims=True)
                sum_v[h] = sum_v[h] * factor + jnp.dot(
                    weights.astype(jnp.bfloat16), kv_v[slot, 1, g], preferred_element_type=jnp.float32
                )
                return inner

            return lax.fori_loop(0, per_group, head, carry, unroll=2)

        lax.fori_loop(0, c - first, source_step, 0)

        def finish(j, carry, g=g):
            h = g * per_group + j
            columns = pl.ds(pl.multiple_of(h * HEAD_DIM, HEAD_DIM), HEAD_DIM)
            out_v[:, columns] = (sum_v[h] / total_v[h]).astype(jnp.bfloat16)
            return carry

        lax.fori_loop(0, per_group, finish, 0)
        out_copy(g).start()

    for g in range(groups):
        for kv in range(2):
            for o in range(1, n_tp):
                remote_copy(c, 0, o, g, kv).wait_send()

            def sent(i, carry, g=g, kv=kv):
                for o in range(n_tp):
                    remote_copy(c + 1 + i, 1 + i, o, g, kv).wait_send()
                return carry

            lax.fori_loop(0, end - 1 - c, sent, 0)
    for g in range(groups):
        out_copy(g).wait()


def per_device(n_long, n_tp, queries, keys_values, segment_ids):
    rows, columns = queries.shape[1:]
    heads = columns // HEAD_DIM
    groups = keys_values.shape[3] // HEAD_DIM // n_tp
    return pl.pallas_call(
        functools.partial(kernel, n_long, n_tp),
        out_shape=jax.ShapeDtypeStruct(queries.shape, queries.dtype),
        in_specs=[
            pl.BlockSpec(memory_space=pl.ANY),
            pl.BlockSpec(memory_space=pl.ANY),
            pl.BlockSpec(memory_space=pltpu.VMEM),
        ],
        out_specs=pl.BlockSpec(memory_space=pl.ANY),
        scratch_shapes=[
            pltpu.VMEM((rows, columns), jnp.bfloat16),
            pltpu.VMEM((n_long, 2, groups, rows, HEAD_DIM), jnp.bfloat16),
            pltpu.VMEM((rows, rows), jnp.float32),
            pltpu.VMEM((heads, rows, HEAD_DIM), jnp.float32),
            pltpu.VMEM((heads, rows, HEAD_DIM), jnp.float32),
            pltpu.VMEM((heads, rows, HEAD_DIM), jnp.float32),
            pltpu.VMEM((rows, columns), jnp.bfloat16),
            pltpu.SemaphoreType.DMA((n_long, n_tp, groups, 2)),
            pltpu.SemaphoreType.DMA((n_long, groups, 2)),
            pltpu.SemaphoreType.DMA((groups,)),
            pltpu.SemaphoreType.DMA((groups,)),
        ],
        compiler_params=pltpu.CompilerParams(
            collective_id=0, has_side_effects=True, vmem_limit_bytes=32 * 1024 * 1024
        ),
    )(queries, keys_values, segment_ids)


def solution(mesh):
    n_long = mesh.shape["ctx"] // 2 + 1
    return jax.shard_map(
        functools.partial(per_device, n_long, mesh.shape["tp"]),
        mesh=mesh,
        in_specs=(
            P(("groups", "dp"), "ctx", "tp"),
            P(("groups", "dp"), None, ("ctx", "tp"), None),
            P(("groups", "dp"), "ctx"),
        ),
        out_specs=P(("groups", "dp"), "ctx", "tp"),
        check_vma=False,
    )
```

profile of v0, /device:TPU:20, one launch (start us, length us, event | category | flops | bytes accessed | tf_op | source)
XLA Modules:
  0.0 30.5 jit_solution(1200305278933354213)
XLA Ops:
  0.0 0.0 copy-start
  0.0 1.2 %copy-done = bf16[1,256,2048]{2,1,0:T(8,128)(2,1)S(1)} copy-done((bf16[1,256,2048]{2,1,0:T(8,128)(2,1)S(1)}, bf16[1,256,2048]{2,1,0:T(8,128)(2,1)}, u32[]{:S(2)}) %copy-start) | copy-done | bytes 1048600
  1.2 0.0 copy-start.1
  1.2 0.9 %copy-done.1 = bf16[1,2,128,512]{3,2,1,0:T(8,128)(2,1)S(1)} copy-done((bf16[1,2,128,512]{3,2,1,0:T(8,128)(2,1)S(1)}, bf16[1,2,128,512]{3,2,1,0:T(8,128)(2,1)}, u32[]{:S(2)}) %copy-start.1) | copy-done | bytes 262168
  2.2 0.0 copy-start.2
  2.2 0.7 %copy-done.2 = s32[1,256]{1,0:T(1,128)S(1)} copy-done((s32[1,256]{1,0:T(1,128)S(1)}, s32[1,256]{1,0:T(1,128)}, u32[]{:S(2)}) %copy-start.2) | copy-done | bytes 1048
  2.9 26.7 %shard_map.37 = bf16[1,256,2048]{2,1,0:T(8,128)(2,1)S(1)} custom-call(bf16[1,256,2048]{2,1,0:T(8,128)(2,1)S(1)} %copy-done, bf16[1,2,128,512]{3,2,1,0:T(8,128)(2,1)S(1)} %copy-done.1, s32[1,256]{1,0:T(1,128)S(1)} %copy-done.2), custom_call_target="tpu_custom_call" | custom-call | tf_op jit(solution)/shard_map/pallas_call | solution.py:177
  29.6 1.0 %copy.5 = bf16[1,256,2048]{2,1,0:T(8,128)(2,1)} copy(bf16[1,256,2048]{2,1,0:T(8,128)(2,1)S(1)} %shard_map.37) | data formatting | bytes 2097152
Async XLA Ops:
  0.0 1.2 %copy-start = (bf16[1,256,2048]{2,1,0:T(8,128)(2,1)S(1)}, bf16[1,256,2048]{2,1,0:T(8,128)(2,1)}, u32[]{:S(2)}) copy-start(bf16[1,256,2048]{2,1,0:T(8,128)(2,1)} %q_ref.1) | copy-start | bytes 3145732
  1.2 0.9 %copy-start.1 = (bf16[1,2,128,512]{3,2,1,0:T(8,128)(2,1)S(1)}, bf16[1,2,128,512]{3,2,1,0:T(8,128)(2,1)}, u32[]{:S(2)}) copy-start(bf16[1,2,128,512]{3,2,1,0:T(8,128)(2,1)} %kv_ref.1) | copy-start | bytes 786436
  2.2 0.7 %copy-start.2 = (s32[1,256]{1,0:T(1,128)S(1)}, s32[1,256]{1,0:T(1,128)}, u32[]{:S(2)}) copy-start(s32[1,256]{1,0:T(1,128)} %seg_ref.1) | copy-start | bytes 3076
where the time goes:
time: 30.8 us; the launch traced here: 30.5 us
  Pallas kernels  26.7 us (87%)
  local copies, waits for them, and re-layouts  3.82 us (12%)
    pallas_call x1, Pallas kernels, per_device(): pl.pallas_call(functools.partial(kernel, n_long, n_tp), out_shape=jax.Sha...  26.7 us
    unnamed x7, local copies, waits for them, and re-layouts  3.82 us

commit v1 on v0

--- a/solution.py
+++ b/solution.py
@@ -13,7 +13,7 @@
 LOG2_SCALE = math.log2(math.e) / math.sqrt(HEAD_DIM)
 
 
-def kernel(n_long, n_tp, q_ref, kv_ref, seg_ref, out_ref, q_v, kv_v, bias_v, top_v, total_v, sum_v, out_v,
+def kernel(n_long, n_tp, q_ref, kv_ref, seg_ref, out_ref, q_v, kv_v, bias_v, flip_v, top_v, total_v, sum_v, out_v,
            send_sem, recv_sem, q_sem, out_sem):
     groups = kv_v.shape[2]
     rows = q_v.shape[0]
@@ -91,10 +91,10 @@
             lax.fori_loop(0, end - 1 - c, send, 0)
 
     seg = seg_ref[...]
-    seg_rows = jnp.transpose(jnp.broadcast_to(seg.astype(jnp.float32), (HEAD_DIM, rows)))[:, :1].astype(jnp.int32)
-    row_index = lax.broadcasted_iota(jnp.int32, (rows, rows), 0)
-    key_index = lax.broadcasted_iota(jnp.int32, (rows, rows), 1)
-    visible = (seg_rows == seg) & (key_index <= row_index)
+    seg_keys = jnp.transpose(jnp.broadcast_to(seg.astype(jnp.float32), (HEAD_DIM, rows)))[:, :1].astype(jnp.int32)
+    key_index = lax.broadcasted_iota(jnp.int32, (rows, rows), 0)
+    row_index = lax.broadcasted_iota(jnp.int32, (rows, rows), 1)
+    visible = (seg_keys == seg) & (key_index <= row_index)
     bias_v[...] = jnp.where(visible, 0.0, -1e30)
 
     def arrived(slot, g, kv):
@@ -103,56 +103,61 @@
 
     def scores_of(h, key_rows):
         q = q_v[:, pl.ds(pl.multiple_of(h * HEAD_DIM, HEAD_DIM), HEAD_DIM)]
-        return lax.dot_general(q, key_rows, (((1,), (1,)), ((), ())), preferred_element_type=jnp.float32) * LOG2_SCALE
+        return lax.dot_general(key_rows, q, (((1,), (1,)), ((), ())), preferred_element_type=jnp.float32) * LOG2_SCALE
+
+    def attend(g, slot, bias, fresh):
+        key_rows = kv_v[slot, 0, g]
+        flip_v[...] = jnp.transpose(kv_v[slot, 1, g])
+        heads_of = [g * per_group + j for j in range(per_group)]
+
+        def add_values(h, weights, factor):
+            product = jnp.dot(flip_v[...], weights, preferred_element_type=jnp.float32)
+            sum_v[h] = product if fresh else sum_v[h] * factor + product
+
+        scores, waiting = scores_of(heads_of[0], key_rows), None
+        for j, h in enumerate(heads_of):
+            following = scores_of(heads_of[j + 1], key_rows) if j + 1 < per_group else None
+            if bias is not None:
+                scores = scores + bias[...]
+            top = jnp.max(scores, axis=0, keepdims=True)
+            factor = None
+            if not fresh:
+                old = top_v[h]
+                top = jnp.maximum(old, top)
+                factor = jnp.exp2(old - top)
+            weights = jnp.exp2(scores - top)
+            total = jnp.sum(weights, axis=0, keepdims=True)
+            top_v[h] = top
+            total_v[h] = total if fresh else total_v[h] * factor + total
+            if waiting is not None:
+                add_values(*waiting)
+            waiting = (h, weights.astype(jnp.bfloat16), factor)
+            scores = following
+        add_values(*waiting)
 
     for g in range(groups):
         q_copy(g).wait()
         arrived(own, g, 0)
         arrived(own, g, 1)
-
-        def own_head(i, carry, g=g):
-            h = g * per_group + i
-            scores = scores_of(h, kv_v[own, 0, g]) + bias_v[...]
-            top = jnp.max(scores, axis=1, keepdims=True)
-            weights = jnp.exp2(scores - top)
-            top_v[h] = jnp.broadcast_to(top, (rows, HEAD_DIM))
-            total_v[h] = jnp.broadcast_to(jnp.sum(weights, axis=1, keepdims=True), (rows, HEAD_DIM))
-            sum_v[h] = jnp.dot(weights.astype(jnp.bfloat16), kv_v[own, 1, g], preferred_element_type=jnp.float32)
-            return carry
-
-        lax.fori_loop(0, per_group, own_head, 0, unroll=2)
+        attend(g, own, bias_v, True)
 
     for g in range(groups):
         def source_step(i, carry, g=g):
             slot = c - 1 - i
             arrived(slot, g, 0)
             arrived(slot, g, 1)
-
-            def head(j, inner):
-                h = g * per_group + j
-                scores = scores_of(h, kv_v[slot, 0, g])
-                old = top_v[h]
-                top = jnp.maximum(old, jnp.max(scores, axis=1, keepdims=True))
-                weights = jnp.exp2(scores - top[:, :1])
-                factor = jnp.exp2(old - top)
-                top_v[h] = top
-                total_v[h] = total_v[h] * factor + jnp.sum(weights, axis=1, keepdims=True)
-                sum_v[h] = sum_v[h] * factor + jnp.dot(
-                    weights.astype(jnp.bfloat16), kv_v[slot, 1, g], preferred_element_type=jnp.float32
-                )
-                return inner
-
-            return lax.fori_loop(0, per_group, head, carry, unroll=2)
+            attend(g, slot, None, False)
+            return carry
 
         lax.fori_loop(0, c - first, source_step, 0)
 
         def finish(j, carry, g=g):
             h = g * per_group + j
             columns = pl.ds(pl.multiple_of(h * HEAD_DIM, HEAD_DIM), HEAD_DIM)
-            out_v[:, columns] = (sum_v[h] / total_v[h]).astype(jnp.bfloat16)
+            out_v[:, columns] = jnp.transpose((sum_v[h] * (1.0 / total_v[h])).astype(jnp.bfloat16))
             return carry
 
-        lax.fori_loop(0, per_group, finish, 0)
+        lax.fori_loop(0, per_group, finish, 0, unroll=2)
         out_copy(g).start()
 
     for g in range(groups):
@@ -170,16 +175,38 @@
         out_copy(g).wait()
 
 
+def place_result(source_ref, out_ref, held, in_sems, out_sems):
+    pieces = in_sems.shape[0]
+    size = source_ref.shape[1] // pieces
+
+    def rows_of(i):
+        return pl.ds(i * size, size)
+
+    def load(i):
+        return pltpu.make_async_copy(source_ref.at[0, rows_of(i)], held.at[rows_of(i)], in_sems.at[i])
+
+    def store(i):
+        return pltpu.make_async_copy(held.at[rows_of(i)], out_ref.at[0, rows_of(i)], out_sems.at[i])
+
+    for i in range(pieces):
+        load(i).start()
+    for i in range(pieces):
+        load(i).wait()
+        store(i).start()
+    for i in range(pieces):
+        store(i).wait()
+
+
 def per_device(n_long, n_tp, queries, keys_values, segment_ids):
     rows, columns = queries.shape[1:]
     heads = columns // HEAD_DIM
     groups = keys_values.shape[3] // HEAD_DIM // n_tp
-    return pl.pallas_call(
+    attended = pl.pallas_call(
         functools.partial(kernel, n_long, n_tp),
         out_shape=jax.ShapeDtypeStruct(queries.shape, queries.dtype),
         in_specs=[
-            pl.BlockSpec(memory_space=pl.ANY),
-            pl.BlockSpec(memory_space=pl.ANY),
+            pl.BlockSpec(memory_space=pltpu.HBM),
+            pl.BlockSpec(memory_space=pltpu.HBM),
             pl.BlockSpec(memory_space=pltpu.VMEM),
         ],
         out_specs=pl.BlockSpec(memory_space=pl.ANY),
@@ -187,9 +214,10 @@
             pltpu.VMEM((rows, columns), jnp.bfloat16),
             pltpu.VMEM((n_long, 2, groups, rows, HEAD_DIM), jnp.bfloat16),
             pltpu.VMEM((rows, rows), jnp.float32),
-            pltpu.VMEM((heads, rows, HEAD_DIM), jnp.float32),
-            pltpu.VMEM((heads, rows, HEAD_DIM), jnp.float32),
-            pltpu.VMEM((heads, rows, HEAD_DIM), jnp.float32),
+            pltpu.VMEM((HEAD_DIM, rows), jnp.bfloat16),
+            pltpu.VMEM((heads, 1, rows), jnp.float32),
+            pltpu.VMEM((heads, 1, rows), jnp.float32),
+            pltpu.VMEM((heads, HEAD_DIM, rows), jnp.float32),
             pltpu.VMEM((rows, columns), jnp.bfloat16),
             pltpu.SemaphoreType.DMA((n_long, n_tp, groups, 2)),
             pltpu.SemaphoreType.DMA((n_long, groups, 2)),
@@ -197,9 +225,21 @@
             pltpu.SemaphoreType.DMA((groups,)),
         ],
         compiler_params=pltpu.CompilerParams(
-            collective_id=0, has_side_effects=True, vmem_limit_bytes=32 * 1024 * 1024
+            collective_id=0, has_side_effects=True, vmem_limit_bytes=60 * 1024 * 1024
         ),
     )(queries, keys_values, segment_ids)
+    return pl.pallas_call(
+        place_result,
+        out_shape=jax.ShapeDtypeStruct(queries.shape, queries.dtype),
+        in_specs=[pl.BlockSpec(memory_space=pl.ANY)],
+        out_specs=pl.BlockSpec(memory_space=pl.ANY),
+        scratch_shapes=[
+            pltpu.VMEM((rows, columns), queries.dtype),
+            pltpu.SemaphoreType.DMA((4,)),
+            pltpu.SemaphoreType.DMA((4,)),
+        ],
+        compiler_params=pltpu.CompilerParams(vmem_limit_bytes=60 * 1024 * 1024),
+    )(attended)
 
 
 def solution(mesh):

time: 30.8 us -> 21.4 us (0.69)
  the two profiles are of different devices: /device:TPU:20 before, /device:TPU:8 now
where the time goes in v1:
time: 21.4 us; the launch traced here: 21.2 us
  Pallas kernels  21.2 us (99%)
    pallas_call x1, Pallas kernels, per_device(): pl.pallas_call(functools.partial(kernel, n_long, n_tp), out_shape=jax.Sha...  19.3 us
    pallas_call x1, Pallas kernels, per_device(): pl.pallas_call(place_result, out_shape=jax.ShapeDtypeStruct(queries.shape...  1.98 us

profile of v1, /device:TPU:8, one launch (start us, length us, event | category | flops | bytes accessed | tf_op | source)
XLA Modules:
  0.0 21.2 jit_solution(12554796144318187602)
XLA Ops:
  0.0 19.3 %shard_map.37.source_ref = bf16[1,256,2048]{2,1,0:T(8,128)(2,1)} custom-call(bf16[1,256,2048]{2,1,0:T(8,128)(2,1)} %q_ref.1, bf16[1,2,128,512]{3,2,1,0:T(8,128)(2,1)} %kv_ref.1, s32[1,256]{1,0:T(1,128)} %seg_ref.1), custom_call_target="tpu_custom_call" | custom-call | tf_op jit(solution)/shard_map/pallas_call | solution.py:204
  19.3 2.0 %shard_map.38 = bf16[1,256,2048]{2,1,0:T(8,128)(2,1)} custom-call(bf16[1,256,2048]{2,1,0:T(8,128)(2,1)} %shard_map.37.source_ref), custom_call_target="tpu_custom_call" | custom-call | tf_op jit(solution)/shard_map/pallas_call | solution.py:231

commit v2 on v1

--- a/solution.py
+++ b/solution.py
@@ -13,8 +13,8 @@
 LOG2_SCALE = math.log2(math.e) / math.sqrt(HEAD_DIM)
 
 
-def kernel(n_long, n_tp, q_ref, kv_ref, seg_ref, out_ref, q_v, kv_v, bias_v, flip_v, top_v, total_v, sum_v, out_v,
-           send_sem, recv_sem, q_sem, out_sem):
+def kernel(n_long, n_tp, q_ref, kv_ref, seg_ref, out_ref, q_v, seg_v, stage_v, kv_v, bias_v, flip_v, top_v, total_v, sum_v,
+           stage_sem, send_sem, recv_sem, q_sem, seg_sem):
     groups = kv_v.shape[2]
     rows = q_v.shape[0]
     part = kv_ref.shape[2]
@@ -33,9 +33,7 @@
         columns = pl.ds(g * width, width)
         return pltpu.make_async_copy(q_ref.at[0, :, columns], q_v.at[:, columns], q_sem.at[g])
 
-    def out_copy(g):
-        columns = pl.ds(g * width, width)
-        return pltpu.make_async_copy(out_v.at[:, columns], out_ref.at[0, :, columns], out_sem.at[g])
+    seg_copy = pltpu.make_async_copy(seg_ref, seg_v, seg_sem)
 
     def partner(o):
         return lax.rem(t + o, n_tp)
@@ -47,12 +45,15 @@
         column = pl.multiple_of((tp_index * groups + g) * HEAD_DIM, HEAD_DIM)
         return kv_ref.at[0, kv, :, pl.ds(column, HEAD_DIM)]
 
+    def stage_copy(tp_index, g, kv):
+        return pltpu.make_async_copy(block(tp_index, g, kv), stage_v.at[kv, g, tp_index], stage_sem.at[kv, g, tp_index])
+
     def local_copy(g, kv):
         return pltpu.make_async_copy(block(t, g, kv), place(g, kv), recv_sem.at[own, g, kv])
 
     def remote_copy(dest, distance, o, g, kv):
         return pltpu.make_async_remote_copy(
-            src_ref=block(partner(o), g, kv),
+            src_ref=stage_v.at[kv, g, partner(o)],
             dst_ref=place(g, kv),
             send_sem=send_sem.at[distance, o, g, kv],
             recv_sem=recv_sem.at[own, g, kv],
@@ -61,6 +62,10 @@
         )
 
     barrier = pltpu.get_barrier_semaphore()
+    for g in range(groups):
+        for kv in range(2):
+            for i in range(n_tp):
+                stage_copy(i, g, kv).start()
     for o in range(1, n_tp):
         pl.semaphore_signal(barrier, inc=1, device_id={"ctx": c, "tp": partner(o)}, device_id_type=MESH)
 
@@ -74,6 +79,11 @@
         for kv in range(2):
             local_copy(g, kv).start()
         q_copy(g).start()
+    seg_copy.start()
+    for g in range(groups):
+        for kv in range(2):
+            for i in range(n_tp):
+                stage_copy(i, g, kv).wait()
     pl.semaphore_wait(barrier, (end - c) * n_tp - 1)
 
     for g in range(groups):
@@ -83,14 +93,15 @@
     for g in range(groups):
         for kv in range(2):
             def send(i, carry, g=g, kv=kv):
-                dest = end - 1 - i
+                dest = c + 1 + i
                 for o in range(n_tp):
                     remote_copy(dest, dest - c, o, g, kv).start()
                 return carry
 
             lax.fori_loop(0, end - 1 - c, send, 0)
 
-    seg = seg_ref[...]
+    seg_copy.wait()
+    seg = seg_v[...]
     seg_keys = jnp.transpose(jnp.broadcast_to(seg.astype(jnp.float32), (HEAD_DIM, rows)))[:, :1].astype(jnp.int32)
     key_index = lax.broadcasted_iota(jnp.int32, (rows, rows), 0)
     row_index = lax.broadcasted_iota(jnp.int32, (rows, rows), 1)
@@ -154,11 +165,10 @@
         def finish(j, carry, g=g):
             h = g * per_group + j
             columns = pl.ds(pl.multiple_of(h * HEAD_DIM, HEAD_DIM), HEAD_DIM)
-            out_v[:, columns] = jnp.transpose((sum_v[h] * (1.0 / total_v[h])).astype(jnp.bfloat16))
+            out_ref[0, :, columns] = jnp.transpose((sum_v[h] * (1.0 / total_v[h])).astype(jnp.bfloat16))
             return carry
 
         lax.fori_loop(0, per_group, finish, 0, unroll=2)
-        out_copy(g).start()
 
     for g in range(groups):
         for kv in range(2):
@@ -171,75 +181,41 @@
                 return carry
 
             lax.fori_loop(0, end - 1 - c, sent, 0)
-    for g in range(groups):
-        out_copy(g).wait()
-
-
-def place_result(source_ref, out_ref, held, in_sems, out_sems):
-    pieces = in_sems.shape[0]
-    size = source_ref.shape[1] // pieces
-
-    def rows_of(i):
-        return pl.ds(i * size, size)
-
-    def load(i):
-        return pltpu.make_async_copy(source_ref.at[0, rows_of(i)], held.at[rows_of(i)], in_sems.at[i])
-
-    def store(i):
-        return pltpu.make_async_copy(held.at[rows_of(i)], out_ref.at[0, rows_of(i)], out_sems.at[i])
-
-    for i in range(pieces):
-        load(i).start()
-    for i in range(pieces):
-        load(i).wait()
-        store(i).start()
-    for i in range(pieces):
-        store(i).wait()
 
 
 def per_device(n_long, n_tp, queries, keys_values, segment_ids):
     rows, columns = queries.shape[1:]
     heads = columns // HEAD_DIM
     groups = keys_values.shape[3] // HEAD_DIM // n_tp
-    attended = pl.pallas_call(
+    return pl.pallas_call(
         functools.partial(kernel, n_long, n_tp),
-        out_shape=jax.ShapeDtypeStruct(queries.shape, queries.dtype),
+        out_shape=pltpu.VMEM(queries.shape, queries.dtype),
         in_specs=[
             pl.BlockSpec(memory_space=pltpu.HBM),
             pl.BlockSpec(memory_space=pltpu.HBM),
-            pl.BlockSpec(memory_space=pltpu.VMEM),
+            pl.BlockSpec(memory_space=pltpu.HBM),
         ],
-        out_specs=pl.BlockSpec(memory_space=pl.ANY),
+        out_specs=pl.BlockSpec(memory_space=pltpu.VMEM),
         scratch_shapes=[
             pltpu.VMEM((rows, columns), jnp.bfloat16),
+            pltpu.VMEM((1, rows), jnp.int32),
+            pltpu.VMEM((2, groups, n_tp, keys_values.shape[2], HEAD_DIM), jnp.bfloat16),
             pltpu.VMEM((n_long, 2, groups, rows, HEAD_DIM), jnp.bfloat16),
             pltpu.VMEM((rows, rows), jnp.float32),
             pltpu.VMEM((HEAD_DIM, rows), jnp.bfloat16),
             pltpu.VMEM((heads, 1, rows), jnp.float32),
             pltpu.VMEM((heads, 1, rows), jnp.float32),
             pltpu.VMEM((heads, HEAD_DIM, rows), jnp.float32),
-            pltpu.VMEM((rows, columns), jnp.bfloat16),
+            pltpu.SemaphoreType.DMA((2, groups, n_tp)),
             pltpu.SemaphoreType.DMA((n_long, n_tp, groups, 2)),
             pltpu.SemaphoreType.DMA((n_long, groups, 2)),
             pltpu.SemaphoreType.DMA((groups,)),
-            pltpu.SemaphoreType.DMA((groups,)),
+            pltpu.SemaphoreType.DMA,
         ],
         compiler_params=pltpu.CompilerParams(
             collective_id=0, has_side_effects=True, vmem_limit_bytes=60 * 1024 * 1024
         ),
     )(queries, keys_values, segment_ids)
-    return pl.pallas_call(
-        place_result,
-        out_shape=jax.ShapeDtypeStruct(queries.shape, queries.dtype),
-        in_specs=[pl.BlockSpec(memory_space=pl.ANY)],
-        out_specs=pl.BlockSpec(memory_space=pl.ANY),
-        scratch_shapes=[
-            pltpu.VMEM((rows, columns), queries.dtype),
-            pltpu.SemaphoreType.DMA((4,)),
-            pltpu.SemaphoreType.DMA((4,)),
-        ],
-        compiler_params=pltpu.CompilerParams(vmem_limit_bytes=60 * 1024 * 1024),
-    )(attended)
 
 
 def solution(mesh):

time: 21.4 us -> 18.6 us (0.87)
  the two profiles are of different devices: /device:TPU:8 before, /device:TPU:20 now
where the time goes in v2:
time: 18.6 us; the launch traced here: 18.5 us
  Pallas kernels  17.5 us (94%)
  local copies, waits for them, and re-layouts  0.97 us (5%)
    pallas_call x1, Pallas kernels, per_device(): pl.pallas_call(functools.partial(kernel, n_long, n_tp), out_shape=pltpu.V...  17.5 us
    unnamed x1, local copies, waits for them, and re-layouts  0.97 us

profile of v2, /device:TPU:20, one launch (start us, length us, event | category | flops | bytes accessed | tf_op | source)
XLA Modules:
  0.0 18.5 jit_solution(11132714103989454864)
XLA Ops:
  0.0 17.5 %shard_map.37 = bf16[1,256,2048]{2,1,0:T(8,128)(2,1)S(1)} custom-call(bf16[1,256,2048]{2,1,0:T(8,128)(2,1)} %q_ref.1, bf16[1,2,128,512]{3,2,1,0:T(8,128)(2,1)} %kv_ref.1, s32[1,256]{1,0:T(1,128)} %seg_ref.1), custom_call_target="tpu_custom_call" | custom-call | tf_op jit(solution)/shard_map/pallas_call | solution.py:190
  17.5 1.0 %copy.5 = bf16[1,256,2048]{2,1,0:T(8,128)(2,1)} copy(bf16[1,256,2048]{2,1,0:T(8,128)(2,1)S(1)} %shard_map.37) | data formatting | bytes 2097152

commit v3 on v2

--- a/solution.py
+++ b/solution.py
@@ -13,7 +13,7 @@
 LOG2_SCALE = math.log2(math.e) / math.sqrt(HEAD_DIM)
 
 
-def kernel(n_long, n_tp, q_ref, kv_ref, seg_ref, out_ref, q_v, seg_v, stage_v, kv_v, bias_v, flip_v, top_v, total_v, sum_v,
+def kernel(n_long, n_tp, q_ref, kv_ref, seg_ref, out_ref, q_v, seg_v, stage_v, kv_v, bias_v, flip_v, top_v, total_v, sum_v, weights_v, factor_v,
            stage_sem, send_sem, recv_sem, q_sem, seg_sem):
     groups = kv_v.shape[2]
     rows = q_v.shape[0]
@@ -118,7 +118,8 @@
 
     def attend(g, slot, bias, fresh):
         key_rows = kv_v[slot, 0, g]
-        flip_v[...] = jnp.transpose(kv_v[slot, 1, g])
+        if fresh:
+            flip_v[...] = jnp.transpose(kv_v[slot, 1, g])
         heads_of = [g * per_group + j for j in range(per_group)]
 
         def add_values(h, weights, factor):
@@ -140,11 +141,21 @@
             total = jnp.sum(weights, axis=0, keepdims=True)
             top_v[h] = top
             total_v[h] = total if fresh else total_v[h] * factor + total
+            scores = following
+            if not fresh:
+                weights_v[j] = weights.astype(jnp.bfloat16)
+                factor_v[j] = factor
+                continue
             if waiting is not None:
                 add_values(*waiting)
             waiting = (h, weights.astype(jnp.bfloat16), factor)
-            scores = following
-        add_values(*waiting)
+        if fresh:
+            add_values(*waiting)
+            return
+        arrived(slot, g, 1)
+        flip_v[...] = jnp.transpose(kv_v[slot, 1, g])
+        for j, h in enumerate(heads_of):
+            add_values(h, weights_v[j], factor_v[j])
 
     for g in range(groups):
         q_copy(g).wait()
@@ -156,7 +167,6 @@
         def source_step(i, carry, g=g):
             slot = c - 1 - i
             arrived(slot, g, 0)
-            arrived(slot, g, 1)
             attend(g, slot, None, False)
             return carry
 
@@ -206,6 +216,8 @@
             pltpu.VMEM((heads, 1, rows), jnp.float32),
             pltpu.VMEM((heads, 1, rows), jnp.float32),
             pltpu.VMEM((heads, HEAD_DIM, rows), jnp.float32),
+            pltpu.VMEM((heads // groups, rows, rows), jnp.bfloat16),
+            pltpu.VMEM((heads // groups, 1, rows), jnp.float32),
             pltpu.SemaphoreType.DMA((2, groups, n_tp)),
             pltpu.SemaphoreType.DMA((n_long, n_tp, groups, 2)),
             pltpu.SemaphoreType.DMA((n_long, groups, 2)),

time: 18.6 us -> 17.8 us (0.957)
  Pallas kernels: 17.5 us -> 16.7 us
    pallas_call x1, Pallas kernels: 17.5 us -> 16.7 us  [per_device(): pl.pallas_call(functools.partial(kernel, n_long, n_tp), out_shape=pltpu.V...]
where the time goes in v3:
time: 17.8 us; the launch traced here: 17.6 us
  Pallas kernels  16.7 us (94%)
  local copies, waits for them, and re-layouts  0.97 us (5%)
    pallas_call x1, Pallas kernels, per_device(): pl.pallas_call(functools.partial(kernel, n_long, n_tp), out_shape=pltpu.V...  16.7 us
    unnamed x1, local copies, waits for them, and re-layouts  0.97 us

profile of v3, /device:TPU:20, one launch (start us, length us, event | category | flops | bytes accessed | tf_op | source)
XLA Modules:
  0.0 17.6 jit_solution(15375629171929586636)
XLA Ops:
  0.0 16.7 %shard_map.37 = bf16[1,256,2048]{2,1,0:T(8,128)(2,1)S(1)} custom-call(bf16[1,256,2048]{2,1,0:T(8,128)(2,1)} %q_ref.1, bf16[1,2,128,512]{3,2,1,0:T(8,128)(2,1)} %kv_ref.1, s32[1,256]{1,0:T(1,128)} %seg_ref.1), custom_call_target="tpu_custom_call" | custom-call | tf_op jit(solution)/shard_map/pallas_call | solution.py:200
  16.7 1.0 %copy.5 = bf16[1,256,2048]{2,1,0:T(8,128)(2,1)} copy(bf16[1,256,2048]{2,1,0:T(8,128)(2,1)S(1)} %shard_map.37) | data formatting | bytes 2097152

commit v4 on v3

--- a/solution.py
+++ b/solution.py
@@ -116,7 +116,10 @@
         q = q_v[:, pl.ds(pl.multiple_of(h * HEAD_DIM, HEAD_DIM), HEAD_DIM)]
         return lax.dot_general(key_rows, q, (((1,), (1,)), ((), ())), preferred_element_type=jnp.float32) * LOG2_SCALE
 
-    def attend(g, slot, bias, fresh):
+    def close(h, summed):
+        out_ref[0, :, h * HEAD_DIM:(h + 1) * HEAD_DIM] = jnp.transpose((summed * (1.0 / total_v[h])).astype(jnp.bfloat16))
+
+    def attend(g, slot, bias, fresh, closing=False):
         key_rows = kv_v[slot, 0, g]
         if fresh:
             flip_v[...] = jnp.transpose(kv_v[slot, 1, g])
@@ -124,7 +127,11 @@
 
         def add_values(h, weights, factor):
             product = jnp.dot(flip_v[...], weights, preferred_element_type=jnp.float32)
-            sum_v[h] = product if fresh else sum_v[h] * factor + product
+            summed = product if fresh else sum_v[h] * factor + product
+            if closing:
+                close(h, summed)
+            else:
+                sum_v[h] = summed
 
         scores, waiting = scores_of(heads_of[0], key_rows), None
         for j, h in enumerate(heads_of):
@@ -170,15 +177,17 @@
             attend(g, slot, None, False)
             return carry
 
-        lax.fori_loop(0, c - first, source_step, 0)
-
-        def finish(j, carry, g=g):
-            h = g * per_group + j
-            columns = pl.ds(pl.multiple_of(h * HEAD_DIM, HEAD_DIM), HEAD_DIM)
-            out_ref[0, :, columns] = jnp.transpose((sum_v[h] * (1.0 / total_v[h])).astype(jnp.bfloat16))
-            return carry
-
-        lax.fori_loop(0, per_group, finish, 0, unroll=2)
+        lax.fori_loop(0, c - first - 1, source_step, 0)
+
+        @pl.when(c > first)
+        def _(g=g):
+            arrived(first, g, 0)
+            attend(g, first, None, False, True)
+
+        @pl.when(c == first)
+        def _(g=g):
+            for j in range(per_group):
+                close(g * per_group + j, sum_v[g * per_group + j])
 
     for g in range(groups):
         for kv in range(2):

time: 17.8 us -> 17.7 us (level)
  Pallas kernels: 16.7 us -> 16.4 us
    pallas_call x1, Pallas kernels: 16.7 us -> 16.4 us  [per_device(): pl.pallas_call(functools.partial(kernel, n_long, n_tp), out_shape=pltpu.V...]
where the time goes in v4:
time: 17.7 us; the launch traced here: 17.4 us
  Pallas kernels  16.4 us (93%)
  local copies, waits for them, and re-layouts  0.97 us (5%)
    pallas_call x1, Pallas kernels, per_device(): pl.pallas_call(functools.partial(kernel, n_long, n_tp), out_shape=pltpu.V...  16.4 us
    unnamed x1, local copies, waits for them, and re-layouts  0.97 us

profile of v4, /device:TPU:20, one launch (start us, length us, event | category | flops | bytes accessed | tf_op | source)
XLA Modules:
  0.0 17.4 jit_solution(147621426519886831)
XLA Ops:
  0.0 16.4 %shard_map.37 = bf16[1,256,2048]{2,1,0:T(8,128)(2,1)S(1)} custom-call(bf16[1,256,2048]{2,1,0:T(8,128)(2,1)} %q_ref.1, bf16[1,2,128,512]{3,2,1,0:T(8,128)(2,1)} %kv_ref.1, s32[1,256]{1,0:T(1,128)} %seg_ref.1), custom_call_target="tpu_custom_call" | custom-call | tf_op jit(solution)/shard_map/pallas_call | solution.py:209
  16.4 1.0 %copy.5 = bf16[1,256,2048]{2,1,0:T(8,128)(2,1)} copy(bf16[1,256,2048]{2,1,0:T(8,128)(2,1)S(1)} %shard_map.37) | data formatting | bytes 2097152
